TPU v7x, 1024 devices: a whole 4x8x16 slice. The times are simulated.
1024 devices in a mesh: gx: 16 (over z), gy: 4 (over x), gz: 16 (over y, core).
Axes of the slice: x: 4, y: 8, z: 16, core: 2. Of those that a mesh axis runs over, the one named last changes fastest.
Arguments:
- right_side: float32 [16, 4, 16, 2, 256], P('gx', 'gy', 'gz'), may hold values from -6 to 6
- hardness: float32 [16, 4, 16, 256], P('gx', 'gy', 'gz'), may hold values from 3 to 8
- coupling: bfloat16 [16, 4, 16, 6, 256, 256], P('gx', 'gy', 'gz'), may hold values from -0.078125 to 0.078125
- coupling_cols: int32 [16, 4, 16, 6], P('gx', 'gy', 'gz'), may hold values from 0 to 26, as said below
- coupling_count: int32 [16, 4, 16], P('gx', 'gy', 'gz'), may hold values from 2 to 6, as said below
- precond_diag: float32 [16, 4, 16, 256], P('gx', 'gy', 'gz'), may hold values from 0.5 to 1.5
- precond: bfloat16 [16, 4, 16, 6, 256, 256], P('gx', 'gy', 'gz'), may hold values from -0.01953125 to 0.01953125
- precond_cols: int32 [16, 4, 16, 6], P('gx', 'gy', 'gz'), may hold values from 0 to 26, as said below
Outputs:
- charges: float32 [16, 4, 16, 2, 256], P('gx', 'gy', 'gz')
- residual: float32 [16, 4, 16, 2, 256], P('gx', 'gy', 'gz')
Inputs may be any that keep to these rules, and one draw needn't show every extreme that they name: `coupling_cols`: each block row's codes are distinct, and slot 0 is always 13, the block itself. `precond_cols`: each block row's codes are distinct, and slot 0 is always 13, the block itself. `coupling_count`: some block row has all 6 slots live.
All inputs are finite; a program needn't handle non-finite values.
Results may differ from a plain program's by a relative error of at most 0.0015.
Values may be sent and summed in bfloat16 or wider, within the bound.
A program may use at most 32 MiB of HBM per device.

v0:
```python
import jax
import jax.numpy as jnp
from jax import lax
from jax.sharding import PartitionSpec as P

ITERS = 2


def with_halo(shard, sides, width):
    for axis, dim in sides:
        count, length = (lax.axis_size(axis), shard.shape[dim])
        up = [(i, (i + 1) % count) for i in range(count)]
        down = [(j, i) for i, j in up]
        last = lax.slice_in_dim(shard, length - width, length, axis=dim)
        initial = lax.slice_in_dim(shard, 0, width, axis=dim)
        before = lax.ppermute(last, axis, up)
        after = lax.ppermute(initial, axis, down)
        shard = jnp.concatenate([before, shard, after], axis=dim)
    return shard


def shifted(block, axis, distance):
    devices = range(lax.axis_size(axis))
    route = [((i - distance) % len(devices), i) for i in devices]
    return lax.ppermute(block, axis, route)


def exchange_rims(vecb):
    return with_halo(vecb, (("gx", 0), ("gy", 1), ("gz", 2)), 1)


def pass_first(plane, offset):
    return shifted(plane, "gx", offset)


def pass_second(plane, offset):
    return shifted(plane, "gy", offset)


def pass_third(plane, offset):
    return shifted(plane, "gz", offset)


def fold_back(spread):
    middle = spread[1:2] + pass_first(spread[0:1], -1) + pass_first(spread[2:3], 1)
    column = middle[:, 1:2] + pass_second(middle[:, 0:1], -1) + pass_second(middle[:, 2:3], 1)
    inside = column[:, :, 1:-1]
    inside = inside.at[:, :, -1:].add(pass_third(column[:, :, 0:1], -1))
    inside = inside.at[:, :, 0:1].add(pass_third(column[:, :, -1:], 1))
    return inside


def slot_places(cols):
    depth = cols.shape[0]
    return (cols // 3, cols % 3 + jnp.arange(depth, dtype=jnp.int32)[:, None])


def gather_slots(extended, cols, live):
    flat = extended.reshape((9,) + extended.shape[2:])
    plane, height = slot_places(cols)
    return flat[plane, height] * live[:, :, None, None].astype(jnp.bfloat16)


def spread_slots(contrib, cols):
    depth = cols.shape[0]
    plane, height = slot_places(cols)
    spread = (
        jnp.zeros((9, depth + 2) + contrib.shape[2:], jnp.float32).at[plane, height].add(contrib)
    )
    return spread.reshape((3, 3, depth + 2) + contrib.shape[2:])


def local_inner(left, right):
    return jnp.sum(left * right, axis=(0, 1, 2, 4))


def precond_inner(left, right):
    return lax.psum(local_inner(left, right), ("gx", "gy", "gz"))


def body(
    right_side,
    hardness,
    coupling,
    coupling_cols,
    coupling_count,
    precond_diag,
    precond,
    precond_cols,
):
    tiles_h = coupling[0, 0]
    tiles_g = precond[0, 0]
    cols_h = coupling_cols[0, 0]
    cols_g = precond_cols[0, 0]
    slots_h = cols_h.shape[1]
    live_h = (jnp.arange(slots_h, dtype=jnp.int32)[None, :] < coupling_count[0, 0][:, None]).astype(
        jnp.float32
    )
    live_g = jnp.ones(cols_g.shape, jnp.float32)
    diag_h = hardness[:, :, :, None, :]
    diag_g = precond_diag[:, :, :, None, :]

    def apply_m(res):
        resb = res.astype(jnp.bfloat16)
        picked = gather_slots(exchange_rims(resb), cols_g, live_g)
        forward = jnp.einsum("zkij,zkrj->zri", tiles_g, picked, preferred_element_type=jnp.float32)
        inter = diag_g * res + forward[None, None]
        interb = inter.astype(jnp.bfloat16)
        contrib = jnp.einsum(
            "zkij,zri->zkrj", tiles_g, interb[0, 0], preferred_element_type=jnp.float32
        )
        return diag_g * inter + fold_back(spread_slots(contrib, cols_g))

    charges = jnp.zeros_like(right_side)
    residual = right_side
    zvec = apply_m(residual)
    direction = zvec
    rz_now = precond_inner(residual, zvec)
    for step in range(ITERS):
        vecb = direction.astype(jnp.bfloat16)
        apply_picked = gather_slots(exchange_rims(vecb), cols_h, live_h)
        apply_forward = jnp.einsum(
            "zkij,zkrj->zri", tiles_h, apply_picked, preferred_element_type=jnp.float32
        )
        apply_contrib = (
            jnp.einsum("zkij,zri->zkrj", tiles_h, vecb[0, 0], preferred_element_type=jnp.float32)
            * live_h[:, :, None, None]
        )
        image = (
            diag_h * direction
            + apply_forward[None, None]
            + fold_back(spread_slots(apply_contrib, cols_h))
        )
        curve = lax.psum(local_inner(direction, image), ("gx", "gy", "gz"))
        alpha = (rz_now / curve)[:, None]
        charges = charges + alpha * direction
        residual = residual - alpha * image
        if step + 1 < ITERS:
            zvec = apply_m(residual)
            rz_next = precond_inner(residual, zvec)
            direction = zvec + (rz_next / rz_now)[:, None] * direction
            rz_now = rz_next
    return (charges, residual)


def solution(mesh):
    placed = (
        P("gx", "gy", "gz", None, None),
        P("gx", "gy", "gz", None),
        P("gx", "gy", "gz", None, None, None),
        P("gx", "gy", "gz", None),
        P("gx", "gy", "gz"),
        P("gx", "gy", "gz", None),
        P("gx", "gy", "gz", None, None, None),
        P("gx", "gy", "gz", None),
    )
    return jax.shard_map(
        body,
        mesh=mesh,
        in_specs=placed,
        out_specs=(P("gx", "gy", "gz", None, None), P("gx", "gy", "gz", None, None)),
        check_vma=False,
    )
```

profile of v0, /device:TPU:1, one launch (start us, length us, event | category | flops | bytes accessed | tf_op | source)
XLA Modules:
  0.0 563.4 jit_solution(9054652017661596169)
XLA Ops:
  1.4 18.8 %collective-permute-start.1 = (bf16[1,1,1,2,256]{4,3,2,1,0:T(2,128)(2,1)S(1)}, bf16[1,1,1,2,256]{4,3,2,1,0:T(2,128)(2,1)S(1)}, u32[]{:S(2)}, u32[]{:S(2)}) collective-permute-start(bf16[1,1,1,2,256]{4,3,2,1,0:T(2,128)(2,1)S(1)} %convert_element_type.40), channel_id=1, source_target_pairs={{64,0},{128,64},{192,128},{256,192},{320,256},{384,320},{448,384},... | collective-permute-start | bytes 3080 | tf_op jit(solution)/shard_map/ppermute | solution.py:17
  22.2 3.5 collective-permute-done
  25.7 4.4 collective-permute-start.3
  32.1 3.6 collective-permute-done.2
  35.7 3.5 collective-permute-start.5
  46.4 4.6 collective-permute-start.6
  53.9 4.6 collective-permute-start.8
  59.2 4.0 collective-permute-start.11
  66.3 5.1 collective-permute-start.13
  74.4 2.5 collective-permute-done.12
  76.9 5.1 collective-permute-start.15
  85.9 4.6 collective-permute-start.18
  90.6 4.2 collective-permute-start.17
  96.7 4.9 collective-permute-start.20
  106.6 126.4 %all-reduce = (f32[2]{0:T(128)S(1)}, f32[2]{0:T(128)S(1)}) all-reduce(f32[2]{0:T(128)S(1)} %get-tuple-element.163, f32[2]{0:T(128)S(1)} %get-tuple-element.162), channel_id=1, replica_groups=mesh['gx'=16,'gy'=4,'gz'=16] {'gx','gy','gz'}, use_global_device_ids=true, to_apply=%region_2.3 | all-reduce | flops 4 | bytes 32 | tf_op jit(solution)/shard_map/psum | solution.py:78
  235.0 3.4 collective-permute-start.24
  240.5 2.4 collective-permute-start.27
  243.0 2.9 collective-permute-start.26
  245.8 2.7 collective-permute-done.26
  248.5 3.3 collective-permute-start.29
  255.1 2.4 collective-permute-start.31
  257.5 4.1 collective-permute-start.30
  264.4 4.6 collective-permute-start.32
  269.7 4.2 collective-permute-start.35
  277.1 125.8 %psum.30 = f32[2]{0:T(128)S(1)} all-reduce(f32[2]{0:T(128)S(1)} %get-tuple-element.170), channel_id=1, replica_groups=mesh['gx'=16,'gy'=4,'gz'=16] {'gx','gy','gz'}, use_global_device_ids=true, to_apply=%region_8.9 | all-reduce | flops 2 | bytes 16 | tf_op jit(solution)/shard_map/psum | solution.py:78
  404.9 3.4 collective-permute-start.36
  412.3 3.4 collective-permute-start.38
  415.7 2.2 collective-permute-start.43
  417.9 4.3 collective-permute-start.42
  422.3 3.0 collective-permute-start.41
  427.2 4.6 collective-permute-start.44
  436.4 126.4 %psum.31 = f32[2]{0:T(128)S(1)} all-reduce(f32[2]{0:T(128)S(1)} %get-tuple-element.166), channel_id=1, replica_groups=mesh['gx'=16,'gy'=4,'gz'=16] {'gx','gy','gz'}, use_global_device_ids=true, to_apply=%region_11.12 | all-reduce | flops 2 | bytes 16 | tf_op jit(solution)/shard_map/psum | solution.py:134
  (152 shorter events, 58.8 us)
Async XLA Ops:
  1.4 20.8 %collective-permute-start.1 = (bf16[1,1,1,2,256]{4,3,2,1,0:T(2,128)(2,1)S(1)}, bf16[1,1,1,2,256]{4,3,2,1,0:T(2,128)(2,1)S(1)}, u32[]{:S(2)}, u32[]{:S(2)}) collective-permute-start(bf16[1,1,1,2,256]{4,3,2,1,0:T(2,128)(2,1)S(1)} %convert_element_type.40), channel_id=1, source_target_pairs={{64,0},{128,64},{192,128},{256,192},{320,256},{384,320},{448,384},... | collective-permute-start | bytes 3080 | tf_op jit(solution)/shard_map/ppermute | solution.py:17
  20.2 5.5 collective-permute-start
  25.7 6.4 %collective-permute-start.3 = (bf16[3,1,1,2,256]{4,3,2,1,0:T(2,128)(2,1)S(1)}, bf16[3,1,1,2,256]{4,3,2,1,0:T(2,128)(2,1)S(1)}, u32[]{:S(2)}, u32[]{:S(2)}) collective-permute-start(bf16[3,1,1,2,256]{4,3,2,1,0:T(2,128)(2,1)S(1)} %pad_maximum_fusion.8), channel_id=1, source_target_pairs={{16,0},{32,16},{48,32},{0,48},{17,1},{33,17},{49,33},{1,49},{18,2}... | collective-permute-start | bytes 9224 | tf_op jit(solution)/shard_map/ppermute | solution.py:17
  30.1 5.6 collective-permute-start.2
  35.7 6.1 %collective-permute-start.5 = (bf16[3,3,1,2,256]{4,3,2,1,0:T(2,128)(2,1)S(1)}, bf16[3,3,1,2,256]{4,3,2,1,0:T(2,128)(2,1)S(1)}, u32[]{:S(2)}, u32[]{:S(2)}) collective-permute-start(bf16[3,3,1,2,256]{4,3,2,1,0:T(2,128)(2,1)S(1)} %pad_maximum_fusion.4), channel_id=1, source_target_pairs={{1,0},{2,1},{3,2},{4,3},{5,4},{6,5},{7,6},{8,7},{9,8},{10,9},{11,1... | collective-permute-start | bytes 27656 | tf_op jit(solution)/shard_map/ppermute | solution.py:17
  44.5 7.2 %collective-permute-start.7 = (f32[1,3,3,2,256]{4,3,2,1,0:T(2,128)S(1)}, f32[1,3,3,2,256]{4,3,2,1,0:T(2,128)S(1)}, u32[]{:S(2)}, u32[]{:S(2)}) collective-permute-start(f32[1,3,3,2,256]{4,3,2,1,0:T(2,128)S(1)} %get-tuple-element.188), channel_id=1, source_target_pairs={{960,0},{0,64},{64,128},{128,192},{192,256},{256,320},{320,384},{3... | collective-permute-start | bytes 55304 | tf_op jit(solution)/shard_map/ppermute | solution.py:25
  46.4 5.4 collective-permute-start.6
  51.9 6.5 %collective-permute-start.9 = (f32[1,1,3,2,256]{4,3,2,1,0:T(2,128)S(1)}, f32[1,1,3,2,256]{4,3,2,1,0:T(2,128)S(1)}, u32[]{:S(2)}, u32[]{:S(2)}) collective-permute-start(f32[1,1,3,2,256]{4,3,2,1,0:T(2,128)S(1)} %get-tuple-element.196), channel_id=1, source_target_pairs={{48,0},{0,16},{16,32},{32,48},{49,1},{1,17},{17,33},{33,49},{50,2}... | collective-permute-start | bytes 18440 | tf_op jit(solution)/shard_map/ppermute | solution.py:25
  66.3 8.1 %collective-permute-start.13 = (bf16[1,1,1,2,256]{4,3,2,1,0:T(2,128)(2,1)S(1)}, bf16[1,1,1,2,256]{4,3,2,1,0:T(2,128)(2,1)S(1)}, u32[]{:S(2)}, u32[]{:S(2)}) collective-permute-start(bf16[1,1,1,2,256]{4,3,2,1,0:T(2,128)(2,1)S(1)} %get-tuple-element.175), channel_id=1, source_target_pairs={{64,0},{128,64},{192,128},{256,192},{320,256},{384,320},{448,384},... | collective-permute-start | bytes 3080 | tf_op jit(solution)/shard_map/ppermute | solution.py:17
  71.4 5.5 collective-permute-start.12
  76.9 13.6 %collective-permute-start.15 = (bf16[3,1,1,2,256]{4,3,2,1,0:T(2,128)(2,1)S(1)}, bf16[3,1,1,2,256]{4,3,2,1,0:T(2,128)(2,1)S(1)}, u32[]{:S(2)}, u32[]{:S(2)}) collective-permute-start(bf16[3,1,1,2,256]{4,3,2,1,0:T(2,128)(2,1)S(1)} %pad_maximum_fusion.9), channel_id=1, source_target_pairs={{16,0},{32,16},{48,32},{0,48},{17,1},{33,17},{49,33},{1,49},{18,2}... | collective-permute-start | bytes 9224 | tf_op jit(solution)/shard_map/ppermute | solution.py:17
  82.1 8.5 %collective-permute-start.14 = (bf16[3,1,1,2,256]{4,3,2,1,0:T(2,128)(2,1)S(1)}, bf16[3,1,1,2,256]{4,3,2,1,0:T(2,128)(2,1)S(1)}, u32[]{:S(2)}, u32[]{:S(2)}) collective-permute-start(bf16[3,1,1,2,256]{4,3,2,1,0:T(2,128)(2,1)S(1)} %pad_maximum_fusion.9), channel_id=1, source_target_pairs={{0,16},{16,32},{32,48},{48,0},{1,17},{17,33},{33,49},{49,1},{2,18}... | collective-permute-start | bytes 9224 | tf_op jit(solution)/shard_map/ppermute | solution.py:16
  84.0 10.7 %collective-permute-start.19 = (f32[1,3,3,2,256]{4,3,2,1,0:T(2,128)S(1)}, f32[1,3,3,2,256]{4,3,2,1,0:T(2,128)S(1)}, u32[]{:S(2)}, u32[]{:S(2)}) collective-permute-start(f32[1,3,3,2,256]{4,3,2,1,0:T(2,128)S(1)} %get-tuple-element.186), channel_id=1, source_target_pairs={{960,0},{0,64},{64,128},{128,192},{192,256},{256,320},{320,384},{3... | collective-permute-start | bytes 55304 | tf_op jit(solution)/shard_map/ppermute | solution.py:25
  85.9 8.8 %collective-permute-start.18 = (f32[1,3,3,2,256]{4,3,2,1,0:T(2,128)S(1)}, f32[1,3,3,2,256]{4,3,2,1,0:T(2,128)S(1)}, u32[]{:S(2)}, u32[]{:S(2)}) collective-permute-start(f32[1,3,3,2,256]{4,3,2,1,0:T(2,128)S(1)} %get-tuple-element.185), channel_id=1, source_target_pairs={{64,0},{128,64},{192,128},{256,192},{320,256},{384,320},{448,384},... | collective-permute-start | bytes 55304 | tf_op jit(solution)/shard_map/ppermute | solution.py:25
  90.6 11.0 %collective-permute-start.17 = (bf16[3,3,1,2,256]{4,3,2,1,0:T(2,128)(2,1)S(1)}, bf16[3,3,1,2,256]{4,3,2,1,0:T(2,128)(2,1)S(1)}, u32[]{:S(2)}, u32[]{:S(2)}) collective-permute-start(bf16[3,3,1,2,256]{4,3,2,1,0:T(2,128)(2,1)S(1)} %pad_maximum_fusion.5), channel_id=1, source_target_pairs={{1,0},{2,1},{3,2},{4,3},{5,4},{6,5},{7,6},{8,7},{9,8},{10,9},{11,1... | collective-permute-start | bytes 27656 | tf_op jit(solution)/shard_map/ppermute | solution.py:17
  94.7 6.8 %collective-permute-start.16 = (bf16[3,3,1,2,256]{4,3,2,1,0:T(2,128)(2,1)S(1)}, bf16[3,3,1,2,256]{4,3,2,1,0:T(2,128)(2,1)S(1)}, u32[]{:S(2)}, u32[]{:S(2)}) collective-permute-start(bf16[3,3,1,2,256]{4,3,2,1,0:T(2,128)(2,1)S(1)} %pad_maximum_fusion.5), channel_id=1, source_target_pairs={{0,1},{1,2},{2,3},{3,4},{4,5},{5,6},{6,7},{7,8},{8,9},{9,10},{10,1... | collective-permute-start | bytes 27656 | tf_op jit(solution)/shard_map/ppermute | solution.py:16
  94.8 7.5 %collective-permute-start.21 = (f32[1,1,3,2,256]{4,3,2,1,0:T(2,128)S(1)}, f32[1,1,3,2,256]{4,3,2,1,0:T(2,128)S(1)}, u32[]{:S(2)}, u32[]{:S(2)}) collective-permute-start(f32[1,1,3,2,256]{4,3,2,1,0:T(2,128)S(1)} %get-tuple-element.194), channel_id=1, source_target_pairs={{48,0},{0,16},{16,32},{32,48},{49,1},{1,17},{17,33},{33,49},{50,2}... | collective-permute-start | bytes 18440 | tf_op jit(solution)/shard_map/ppermute | solution.py:25
  96.7 5.6 collective-permute-start.20
  235.0 5.5 collective-permute-start.24
  243.0 5.6 collective-permute-start.26
  255.1 6.5 %collective-permute-start.31 = (f32[1,3,3,2,256]{4,3,2,1,0:T(2,128)S(1)}, f32[1,3,3,2,256]{4,3,2,1,0:T(2,128)S(1)}, u32[]{:S(2)}, u32[]{:S(2)}) collective-permute-start(f32[1,3,3,2,256]{4,3,2,1,0:T(2,128)S(1)} %get-tuple-element.184), channel_id=1, source_target_pairs={{960,0},{0,64},{64,128},{128,192},{192,256},{256,320},{320,384},{3... | collective-permute-start | bytes 55304 | tf_op jit(solution)/shard_map/ppermute | solution.py:25
  262.5 6.5 %collective-permute-start.33 = (f32[1,1,3,2,256]{4,3,2,1,0:T(2,128)S(1)}, f32[1,1,3,2,256]{4,3,2,1,0:T(2,128)S(1)}, u32[]{:S(2)}, u32[]{:S(2)}) collective-permute-start(f32[1,1,3,2,256]{4,3,2,1,0:T(2,128)S(1)} %get-tuple-element.192), channel_id=1, source_target_pairs={{48,0},{0,16},{16,32},{32,48},{49,1},{1,17},{17,33},{33,49},{50,2}... | collective-permute-start | bytes 18440 | tf_op jit(solution)/shard_map/ppermute | solution.py:25
  269.7 6.1 %collective-permute-start.35 = (f32[1,1,1,2,256]{4,3,2,1,0:T(2,128)S(1)}, f32[1,1,1,2,256]{4,3,2,1,0:T(2,128)S(1)}, u32[]{:S(2)}, u32[]{:S(2)}) collective-permute-start(f32[1,1,1,2,256]{4,3,2,1,0:T(2,128)S(1)} %get-tuple-element.200), channel_id=1, source_target_pairs={{15,0},{0,1},{1,2},{2,3},{3,4},{4,5},{5,6},{6,7},{7,8},{8,9},{9,10... | collective-permute-start | bytes 6152 | tf_op jit(solution)/shard_map/ppermute | solution.py:25
  402.9 6.4 %collective-permute-start.37 = (bf16[1,1,1,2,256]{4,3,2,1,0:T(2,128)(2,1)S(1)}, bf16[1,1,1,2,256]{4,3,2,1,0:T(2,128)(2,1)S(1)}, u32[]{:S(2)}, u32[]{:S(2)}) collective-permute-start(bf16[1,1,1,2,256]{4,3,2,1,0:T(2,128)(2,1)S(1)} %get-tuple-element.168), channel_id=1, source_target_pairs={{64,0},{128,64},{192,128},{256,192},{320,256},{384,320},{448,384},... | collective-permute-start | bytes 3080 | tf_op jit(solution)/shard_map/ppermute | solution.py:17
  404.9 5.5 collective-permute-start.36
  410.4 11.8 %collective-permute-start.39 = (bf16[3,1,1,2,256]{4,3,2,1,0:T(2,128)(2,1)S(1)}, bf16[3,1,1,2,256]{4,3,2,1,0:T(2,128)(2,1)S(1)}, u32[]{:S(2)}, u32[]{:S(2)}) collective-permute-start(bf16[3,1,1,2,256]{4,3,2,1,0:T(2,128)(2,1)S(1)} %pad_maximum_fusion.11), channel_id=1, source_target_pairs={{16,0},{32,16},{48,32},{0,48},{17,1},{33,17},{49,33},{1,49},{18,2}... | collective-permute-start | bytes 9224 | tf_op jit(solution)/shard_map/ppermute | solution.py:17
  412.3 9.9 %collective-permute-start.38 = (bf16[3,1,1,2,256]{4,3,2,1,0:T(2,128)(2,1)S(1)}, bf16[3,1,1,2,256]{4,3,2,1,0:T(2,128)(2,1)S(1)}, u32[]{:S(2)}, u32[]{:S(2)}) collective-permute-start(bf16[3,1,1,2,256]{4,3,2,1,0:T(2,128)(2,1)S(1)} %pad_maximum_fusion.11), channel_id=1, source_target_pairs={{0,16},{16,32},{32,48},{48,0},{1,17},{17,33},{33,49},{49,1},{2,18}... | collective-permute-start | bytes 9224 | tf_op jit(solution)/shard_map/ppermute | solution.py:16
  415.7 9.5 %collective-permute-start.43 = (f32[1,3,3,2,256]{4,3,2,1,0:T(2,128)S(1)}, f32[1,3,3,2,256]{4,3,2,1,0:T(2,128)S(1)}, u32[]{:S(2)}, u32[]{:S(2)}) collective-permute-start(f32[1,3,3,2,256]{4,3,2,1,0:T(2,128)S(1)} %get-tuple-element.182), channel_id=1, source_target_pairs={{960,0},{0,64},{64,128},{128,192},{192,256},{256,320},{320,384},{3... | collective-permute-start | bytes 55304 | tf_op jit(solution)/shard_map/ppermute | solution.py:25
  417.9 7.4 %collective-permute-start.42 = (f32[1,3,3,2,256]{4,3,2,1,0:T(2,128)S(1)}, f32[1,3,3,2,256]{4,3,2,1,0:T(2,128)S(1)}, u32[]{:S(2)}, u32[]{:S(2)}) collective-permute-start(f32[1,3,3,2,256]{4,3,2,1,0:T(2,128)S(1)} %get-tuple-element.181), channel_id=1, source_target_pairs={{64,0},{128,64},{192,128},{256,192},{320,256},{384,320},{448,384},... | collective-permute-start | bytes 55304 | tf_op jit(solution)/shard_map/ppermute | solution.py:25
  422.3 9.5 %collective-permute-start.41 = (bf16[3,3,1,2,256]{4,3,2,1,0:T(2,128)(2,1)S(1)}, bf16[3,3,1,2,256]{4,3,2,1,0:T(2,128)(2,1)S(1)}, u32[]{:S(2)}, u32[]{:S(2)}) collective-permute-start(bf16[3,3,1,2,256]{4,3,2,1,0:T(2,128)(2,1)S(1)} %pad_maximum_fusion.7), channel_id=1, source_target_pairs={{1,0},{2,1},{3,2},{4,3},{5,4},{6,5},{7,6},{8,7},{9,8},{10,9},{11,1... | collective-permute-start | bytes 27656 | tf_op jit(solution)/shard_map/ppermute | solution.py:17
  425.2 6.6 %collective-permute-start.40 = (bf16[3,3,1,2,256]{4,3,2,1,0:T(2,128)(2,1)S(1)}, bf16[3,3,1,2,256]{4,3,2,1,0:T(2,128)(2,1)S(1)}, u32[]{:S(2)}, u32[]{:S(2)}) collective-permute-start(bf16[3,3,1,2,256]{4,3,2,1,0:T(2,128)(2,1)S(1)} %pad_maximum_fusion.7), channel_id=1, source_target_pairs={{0,1},{1,2},{2,3},{3,4},{4,5},{5,6},{6,7},{7,8},{8,9},{9,10},{10,1... | collective-permute-start | bytes 27656 | tf_op jit(solution)/shard_map/ppermute | solution.py:16
  425.3 7.2 %collective-permute-start.45 = (f32[1,1,3,2,256]{4,3,2,1,0:T(2,128)S(1)}, f32[1,1,3,2,256]{4,3,2,1,0:T(2,128)S(1)}, u32[]{:S(2)}, u32[]{:S(2)}) collective-permute-start(f32[1,1,3,2,256]{4,3,2,1,0:T(2,128)S(1)} %get-tuple-element.190), channel_id=1, source_target_pairs={{48,0},{0,16},{16,32},{32,48},{49,1},{1,17},{17,33},{33,49},{50,2}... | collective-permute-start | bytes 18440 | tf_op jit(solution)/shard_map/ppermute | solution.py:25
  (23 other events, 168.2 us)
where the time goes:
time: 565 us; the launch traced here: 563 us
  blocking collectives  379 us (67%)
  starting transfers between devices  145 us (26%)
  waiting for transfers between devices  26.5 us (5%)
  other arithmetic  5.73 us (1%)
    psum x2, blocking collectives, precond_inner(): return lax.psum(local_inner(left, right), ('gx', 'gy', 'gz'))  252 us
    psum x1, blocking collectives, body(): curve = lax.psum(local_inner(direction, image), ('gx', 'gy', 'gz'))  126 us
    ppermute x24, starting transfers between devices, shifted(): return lax.ppermute(block, axis, route)  67.2 us
    ppermute x12, starting transfers between devices, with_halo(): after = lax.ppermute(initial, axis, down)  55.6 us
    ppermute x12, starting transfers between devices, with_halo(): before = lax.ppermute(last, axis, up)  21.8 us
    ppermute x12, waiting for transfers between devices, with_halo(): before = lax.ppermute(last, axis, up)  15.9 us
  transfers between devices with their start and end apart: 48, of which 23 were waited for; matrix products, arithmetic and copies ran while one was open for 1% of the time, Pallas kernels for 0%

commit v1 on v0

v1 whole, which is shorter than its diff:
```python
import jax
import jax.numpy as jnp
from jax import lax
from jax.experimental import pallas as pl
from jax.experimental.pallas import tpu as pltpu
from jax.sharding import PartitionSpec as P

SYS = 2
BS = 256
SLOTS = 6
CODES = 27
SELF = 13
AXES = ("gx", "gy", "gz")
MESH = pl.DeviceIdType.MESH
NEAR = sorted(
    (o for o in range(CODES) if o != SELF),
    key=lambda o: -(abs(o // 9 - 1) + abs(o // 3 % 3 - 1) + abs(o % 3 - 1)),
)


def dot_fwd(vec, tile):
    return lax.dot_general(vec, tile, (((1,), (1,)), ((), ())), preferred_element_type=jnp.float32)


def dot_bwd(vec, tile):
    return lax.dot_general(vec, tile, (((1,), (0,)), ((), ())), preferred_element_type=jnp.float32)


def kernel(
    sizes,
    rhs_hbm, hard_hbm, coup_hbm, ccol_hbm, ccnt_hbm, pdia_hbm, prec_hbm, pcol_hbm,
    charges_hbm, resid_hbm,
    rhs, hard, coup, pdia, prec, ccol, ccnt, pcol,
    inv_g, inv_h, sel_h,
    halo_a, send_b, fold_b, send_c, both_c, send_d, halo_d, send_e, fold_e, send_f, both_f,
    parts, part_gx, part_gz, part_gy, sums_x, sums_z,
    terms, out_c, out_r,
    load_sem, send_sem, recv_sem,
):
    me = [lax.axis_index(a) for a in AXES]
    steps = [
        [lax.rem(me[a] + (n - 1), n), me[a], lax.rem(me[a] + 1, n)] for a, n in enumerate(sizes)
    ]

    def near(code):
        return (steps[0][code // 9], steps[1][code // 3 % 3], steps[2][code % 3])

    def along(axis, distance):
        place = list(me)
        place[axis] = lax.rem(me[axis] + distance, sizes[axis])
        return tuple(place)

    loads = [
        pltpu.make_async_copy(source, target, load_sem.at[i])
        for i, (source, target) in enumerate((
            (rhs_hbm, rhs), (pcol_hbm, pcol), (ccol_hbm, ccol), (ccnt_hbm, ccnt), (pdia_hbm, pdia),
            (prec_hbm, prec), (hard_hbm, hard), (coup_hbm, coup),
        ))
    ]
    for load in loads:
        load.start()

    barrier = pltpu.get_barrier_semaphore()
    partners = 0
    for axis, n in enumerate(sizes):
        for distance in range(2, n - 1):
            pl.semaphore_signal(barrier, inc=1, device_id=along(axis, distance), device_id_type=MESH)
            partners += 1
    for code in NEAR:
        pl.semaphore_signal(barrier, inc=1, device_id=near(code), device_id_type=MESH)
        partners += 1

    zero = jnp.zeros((SYS, BS), jnp.float32)
    terms[SLOTS] = zero
    both_c[CODES, 0:SYS] = zero
    both_f[CODES, 0:SYS] = zero

    for load in loads[:4]:
        load.wait()
    halo_a[SELF] = rhs[...]
    codes_g = [pcol[0, k] for k in range(SLOTS)]
    count = ccnt[0, 0]
    codes_h = [ccol[0, k] for k in range(SLOTS)]
    for k in range(SLOTS):
        sel_h[k] = jnp.where(k < count, codes_h[k], CODES)
    codes_h = [sel_h[k] for k in range(SLOTS)]
    for inv, codes in ((inv_g, codes_g), (inv_h, codes_h)):
        for code in NEAR:
            slot = jnp.int32(SLOTS)
            for k in range(1, SLOTS):
                slot = jnp.where(codes[k] == code, k, slot)
            inv[code] = slot

    pl.semaphore_wait(barrier, partners)

    def exchange(phase, source_of, target):
        for code in NEAR:
            pltpu.make_async_remote_copy(
                src_ref=source_of(code),
                dst_ref=target.at[CODES - 1 - code],
                send_sem=send_sem.at[phase],
                recv_sem=recv_sem.at[phase],
                device_id=near(code),
                device_id_type=MESH,
            ).start()

    def arrived(phase, target, n):
        here = target.at[pl.ds(0, n)]
        pltpu.make_async_copy(here, here, recv_sem.at[phase]).wait()

    def left(phase, target, n):
        here = target.at[pl.ds(0, n)]
        pltpu.make_async_copy(here, here, send_sem.at[phase]).wait()

    def forward(tiles, codes, halo, rows):
        total = None
        for k in range(SLOTS):
            picked = halo[SELF, rows] if k == 0 else halo[codes[k], rows]
            term = dot_fwd(picked.astype(jnp.bfloat16), tiles[k])
            total = term if total is None else total + term
        return total

    def backward(tiles, vecb):
        own = dot_bwd(vecb, tiles[0])
        for k in range(1, SLOTS):
            terms[k] = dot_bwd(vecb, tiles[k])
        return own

    def folded(fold, rows):
        total = None
        for code in NEAR:
            term = fold[code, rows]
            total = term if total is None else total + term
        return total

    def inner(left_vec, right_vec):
        return jnp.sum(left_vec * right_vec, axis=1, keepdims=True)

    everything = slice(0, SYS)
    second = slice(SYS, 2 * SYS)

    def apply_m_tail(vec, halo, send, fold, phase):
        inter = pdia[...] * vec + forward(prec, codes_g, halo, everything)
        own = backward(prec, inter.astype(jnp.bfloat16))
        for code in NEAR:
            send[code] = terms[inv_g[code]]
        exchange(phase, lambda code: send.at[code], fold)
        partial = pdia[...] * inter + own
        arrived(phase, fold, CODES - 1)
        return partial + folded(fold, everything)

    def apply_h(vec, send, both, phase):
        own = backward(coup, vec.astype(jnp.bfloat16))
        for code in NEAR:
            send[code, everything] = vec
            send[code, second] = terms[inv_h[code]]
        exchange(phase, lambda code: send.at[code], both)
        both[SELF, everything] = vec
        partial = hard[...] * vec + own
        arrived(phase, both, CODES - 1)
        return partial + folded(both, second) + forward(coup, codes_h, both, everything)

    r0 = rhs[...]
    exchange(0, lambda code: rhs, halo_a)
    for load in loads[4:6]:
        load.wait()
    arrived(0, halo_a, CODES - 1)
    z0 = apply_m_tail(r0, halo_a, send_b, fold_b, 1)
    for load in loads[6:]:
        load.wait()
    w0 = apply_h(z0, send_c, both_c, 2)
    send_d[...] = w0
    halo_d[SELF] = w0
    exchange(3, lambda code: send_d, halo_d)
    lane = lax.broadcasted_iota(jnp.int32, (SYS, 128), 1)

    def placed(pairs):
        total = jnp.zeros((SYS, 128), jnp.float32)
        for place, value in pairs:
            total = jnp.where(lane == place, value, total)
        return total

    known = placed(((0, inner(r0, z0)), (1, inner(z0, w0))))
    arrived(3, halo_d, CODES - 1)
    y0 = apply_m_tail(w0, halo_d, send_e, fold_e, 4)
    q0 = apply_h(y0, send_f, both_f, 5)
    known = jnp.where(lane == 2, inner(w0, y0), known)
    known = jnp.where(lane == 3, inner(r0, y0), known)
    known = jnp.where(lane == 4, inner(y0, q0), known)

    parts[...] = known
    source, total = parts, known
    for stage, (axis, slots) in enumerate(((0, part_gx), (2, part_gz), (1, part_gy))):
        n, phase = sizes[axis], 6 + stage
        for distance in range(1, n):
            pltpu.make_async_remote_copy(
                src_ref=source,
                dst_ref=slots.at[distance - 1],
                send_sem=send_sem.at[phase],
                recv_sem=recv_sem.at[phase],
                device_id=along(axis, distance),
                device_id_type=MESH,
            ).start()
        arrived(phase, slots, n - 1)
        for distance in range(1, n):
            total = total + slots[distance - 1]
        if stage < 2:
            source = (sums_x, sums_z)[stage]
            source[...] = total

    rz0, c0, wy, ry, yq = (total[:, i : i + 1] for i in range(5))
    alpha = rz0 / c0
    rz1 = rz0 - alpha * (ry + c0) + alpha * alpha * wy
    scale = 1.0 + rz1 / rz0
    c1 = scale * scale * c0 - 2.0 * alpha * scale * wy + alpha * alpha * yq
    alpha1 = rz1 / c1
    out_c[...] = alpha * z0 + alpha1 * (scale * z0 - alpha * y0)
    out_r[...] = r0 - alpha * w0 - alpha1 * (scale * w0 - alpha * q0)
    outs = [
        pltpu.make_async_copy(out_c, charges_hbm, load_sem.at[0]),
        pltpu.make_async_copy(out_r, resid_hbm, load_sem.at[1]),
    ]
    for out in outs:
        out.start()
    for phase, target in ((0, halo_a), (1, fold_b), (2, both_c), (3, halo_d), (4, fold_e), (5, both_f)):
        left(phase, target, CODES - 1)
    for phase, target in ((6, part_gx), (7, part_gz), (8, part_gy)):
        left(phase, target, target.shape[0])
    for out in outs:
        out.wait()


def body(sizes, right_side, hardness, coupling, coupling_cols, coupling_count, precond_diag, precond, precond_cols):
    f32, i32, bf16 = jnp.float32, jnp.int32, jnp.bfloat16
    vec = jax.ShapeDtypeStruct((SYS, BS), f32)
    slots = lambda n, rows=SYS: pltpu.VMEM((n, rows, BS), f32)
    anywhere = pl.BlockSpec(memory_space=pl.ANY)

    def run(*refs):
        kernel(sizes, *refs)

    charges, residual = pl.pallas_call(
        run,
        out_shape=(vec, vec),
        in_specs=[anywhere] * 8,
        out_specs=(anywhere, anywhere),
        scratch_shapes=[
            pltpu.VMEM((SYS, BS), f32), pltpu.VMEM((1, BS), f32), pltpu.VMEM((SLOTS, BS, BS), bf16),
            pltpu.VMEM((1, BS), f32), pltpu.VMEM((SLOTS, BS, BS), bf16),
            pltpu.SMEM((1, SLOTS), i32), pltpu.SMEM((1, 1), i32), pltpu.SMEM((1, SLOTS), i32),
            pltpu.SMEM((CODES,), i32), pltpu.SMEM((CODES,), i32), pltpu.SMEM((SLOTS,), i32),
            slots(CODES), slots(CODES), slots(CODES), slots(CODES, 2 * SYS), slots(CODES + 1, 2 * SYS),
            pltpu.VMEM((SYS, BS), f32), slots(CODES), slots(CODES), slots(CODES), slots(CODES, 2 * SYS), slots(CODES + 1, 2 * SYS),
            pltpu.VMEM((SYS, 128), f32), pltpu.VMEM((sizes[0] - 1, SYS, 128), f32), pltpu.VMEM((sizes[2] - 1, SYS, 128), f32),
            pltpu.VMEM((sizes[1] - 1, SYS, 128), f32), pltpu.VMEM((SYS, 128), f32), pltpu.VMEM((SYS, 128), f32),
            slots(SLOTS + 1), pltpu.VMEM((SYS, BS), f32), pltpu.VMEM((SYS, BS), f32),
            pltpu.SemaphoreType.DMA((8,)), pltpu.SemaphoreType.DMA((9,)), pltpu.SemaphoreType.DMA((9,)),
        ],
        compiler_params=pltpu.CompilerParams(
            collective_id=0, has_side_effects=True, vmem_limit_bytes=32 * 1024 * 1024
        ),
    )(
        right_side.reshape(SYS, BS), hardness.reshape(1, BS), coupling.reshape(SLOTS, BS, BS),
        coupling_cols.reshape(1, SLOTS), coupling_count.reshape(1, 1), precond_diag.reshape(1, BS),
        precond.reshape(SLOTS, BS, BS), precond_cols.reshape(1, SLOTS),
    )
    return charges.reshape(right_side.shape), residual.reshape(right_side.shape)


def solution(mesh):
    sizes = tuple(mesh.shape[a] for a in AXES)
    placed = (
        P("gx", "gy", "gz", None, None),
        P("gx", "gy", "gz", None),
        P("gx", "gy", "gz", None, None, None),
        P("gx", "gy", "gz", None),
        P("gx", "gy", "gz"),
        P("gx", "gy", "gz", None),
        P("gx", "gy", "gz", None, None, None),
        P("gx", "gy", "gz", None),
    )
    return jax.shard_map(
        lambda *args: body(sizes, *args),
        mesh=mesh,
        in_specs=placed,
        out_specs=(P("gx", "gy", "gz", None, None), P("gx", "gy", "gz", None, None)),
        check_vma=False,
    )
```

time: 565 us -> 77.8 us (0.14)
  blocking collectives: 379 us -> 0 us
  starting transfers between devices: 145 us -> 0 us
  Pallas kernels: 0 us -> 72.1 us
  waiting for transfers between devices: 26.5 us -> 0 us
  other arithmetic: 5.73 us -> 0 us
    psum x3 -> x0, blocking collectives: 379 us -> none  [the longest x2 252 us: precond_inner(): return lax.psum(local_inner(left, right), ('gx', 'gy', 'gz'))]
    ppermute x48 -> x0, starting transfers between devices: 145 us -> none  [the longest x24 67.2 us: shifted(): return lax.ppermute(block, axis, route)]
    pallas_call x0 -> x1, Pallas kernels: none -> 72.1 us  [body(): pl.pallas_call(run, out_shape=(vec, vec), in_specs=[anywhere] * 8, out_sp...]
    ppermute x48 -> x0, waiting for transfers between devices: 26.5 us -> none  [the longest x12 15.9 us: with_halo(): before = lax.ppermute(last, axis, up)]
  transfers between devices with their start and end apart: 48 -> 0, of which waited for: 23 -> 0; matrix products, arithmetic and copies ran while one was open for 1% -> 0% of each run, Pallas kernels for 0% -> 0%
where the time goes in v1:
time: 77.8 us; the launch traced here: 77.6 us
  Pallas kernels  72.1 us (93%)
  local copies, waits for them, and re-layouts  4.11 us (5%)
  between operations  1.33 us (2%)
    pallas_call x1, Pallas kernels, body(): pl.pallas_call(run, out_shape=(vec, vec), in_specs=[anywhere] * 8, out_sp...  72.1 us
    unnamed x16, local copies, waits for them, and re-layouts  4.11 us

profile of v1, /device:TPU:1, one launch (start us, length us, event | category | flops | bytes accessed | tf_op | source)
XLA Modules:
  0.0 77.6 jit_solution(6635869013102982922)
XLA Ops:
  1.3 0.0 copy-start.4
  1.3 0.0 copy-start.6
  1.3 0.0 copy-start.2
  1.3 0.0 copy-start.3
  1.3 0.0 copy-start.5
  1.3 0.6 copy-done.4
  2.0 0.0 copy-done.6
  2.0 0.0 copy-done.2
  2.0 0.0 copy-done.3
  2.0 0.0 copy-done.5
  2.0 0.0 copy-start
  2.0 1.1 %copy-done = bf16[1,1,1,6,256,256]{5,4,3,2,1,0:T(8,128)(2,1)S(1)} copy-done((bf16[1,1,1,6,256,256]{5,4,3,2,1,0:T(8,128)(2,1)S(1)}, bf16[1,1,1,6,256,256]{5,4,3,2,1,0:T(8,128)(2,1)}, u32[]{:S(2)}) %copy-start) | copy-done | bytes 786456
  3.1 0.0 copy-start.1
  3.1 1.1 %copy-done.1 = bf16[1,1,1,6,256,256]{5,4,3,2,1,0:T(8,128)(2,1)S(1)} copy-done((bf16[1,1,1,6,256,256]{5,4,3,2,1,0:T(8,128)(2,1)S(1)}, bf16[1,1,1,6,256,256]{5,4,3,2,1,0:T(8,128)(2,1)}, u32[]{:S(2)}) %copy-start.1) | copy-done | bytes 786456
  4.3 72.1 %shard_map.95 = (f32[2,256]{1,0:T(2,128)S(1)}, f32[2,256]{1,0:T(2,128)S(1)}) custom-call(f32[2,256]{1,0:T(2,128)S(1)} %bitcast.13, f32[1,256]{1,0:T(1,128)S(1)} %bitcast.16, bf16[6,256,256]{2,1,0:T(8,128)(2,1)S(1)} %bitcast.11, s32[1,6]{1,0:T(1,128)S(1)} %bitcast.18, s32[1,1]{1,0:T(1,128)} %bitcast.10.refs_4_, f32[1,256]{1,0:T(1,128)S(1)} %bitcast.17, ...), custom_call_target="tpu_custom_call" | custom-call | tf_op jit(solution)/shard_map/pallas_call | solution.py:242
  76.4 0.6 copy.13
  77.0 0.6 copy.14
Async XLA Ops:
  1.3 0.7 copy-start.4
  1.3 0.7 copy-start.6
  1.3 0.7 copy-start.2
  1.3 0.7 copy-start.3
  1.3 0.7 copy-start.5
  2.0 1.1 %copy-start = (bf16[1,1,1,6,256,256]{5,4,3,2,1,0:T(8,128)(2,1)S(1)}, bf16[1,1,1,6,256,256]{5,4,3,2,1,0:T(8,128)(2,1)}, u32[]{:S(2)}) copy-start(bf16[1,1,1,6,256,256]{5,4,3,2,1,0:T(8,128)(2,1)} %param.10) | copy-start | bytes 2359300
  3.1 1.1 %copy-start.1 = (bf16[1,1,1,6,256,256]{5,4,3,2,1,0:T(8,128)(2,1)S(1)}, bf16[1,1,1,6,256,256]{5,4,3,2,1,0:T(8,128)(2,1)}, u32[]{:S(2)}) copy-start(bf16[1,1,1,6,256,256]{5,4,3,2,1,0:T(8,128)(2,1)} %param.14) | copy-start | bytes 2359300

commit v2 on v1

v2 whole, which is shorter than its diff:
```python
import jax
import jax.numpy as jnp
from jax import lax
from jax.experimental import pallas as pl
from jax.experimental.pallas import tpu as pltpu
from jax.sharding import PartitionSpec as P

SYS = 2
BS = 256
SLOTS = 6
CODES = 27
SELF = 13
AXES = ("gx", "gy", "gz")
MESH = pl.DeviceIdType.MESH
NEAR = sorted(
    (o for o in range(CODES) if o != SELF),
    key=lambda o: -(abs(o // 9 - 1) + abs(o // 3 % 3 - 1) + abs(o % 3 - 1)),
)


FURTHER = ((-2, 0, 0), (2, 0, 0), (0, 0, -2), (0, 0, 2))
SUMS = 5


def two_parts(vec):
    rest = vec - vec.astype(jnp.bfloat16).astype(jnp.float32)
    return jnp.concatenate([vec, rest], axis=0).astype(jnp.bfloat16)


def joined(product):
    return product[0:SYS] + product[SYS : 2 * SYS]


def dot_fwd(vec, tile):
    return lax.dot_general(vec, tile, (((1,), (1,)), ((), ())), preferred_element_type=jnp.float32)


def dot_bwd(vec, tile):
    return lax.dot_general(vec, tile, (((1,), (0,)), ((), ())), preferred_element_type=jnp.float32)


def kernel(
    sizes,
    rhs_hbm, hard_hbm, coup_hbm, ccol_hbm, ccnt_hbm, pdia_hbm, prec_hbm, pcol_hbm,
    charges, resid,
    rhs, hard, coup, pdia, prec, ccol, ccnt, pcol,
    inv_g, inv_h, sel_h,
    halo_a, send_b, fold_b, send_c, both_c, send_d, halo_d, send_e, fold_e, send_f, both_f,
    parts, part_plane, part_ring, sums_plane,
    terms,
    load_sem, send_sem, recv_sem,
):
    me = [lax.axis_index(a) for a in AXES]
    steps = [
        [lax.rem(me[a] + (n - 1), n), me[a], lax.rem(me[a] + 1, n)] for a, n in enumerate(sizes)
    ]

    def near(code):
        return (steps[0][code // 9], steps[1][code // 3 % 3], steps[2][code % 3])

    def away(distances):
        return tuple(
            m if d == 0 else lax.rem(m + d % n, n) for m, d, n in zip(me, distances, sizes)
        )

    loads = [
        pltpu.make_async_copy(source, target, load_sem.at[i])
        for i, (source, target) in enumerate((
            (rhs_hbm, rhs), (pcol_hbm, pcol), (ccol_hbm, ccol), (ccnt_hbm, ccnt), (pdia_hbm, pdia),
            (prec_hbm, prec), (hard_hbm, hard), (coup_hbm, coup),
        ))
    ]
    for load in loads:
        load.start()

    barrier = pltpu.get_barrier_semaphore()
    for code in NEAR:
        pl.semaphore_signal(barrier, inc=1, device_id=near(code), device_id_type=MESH)
    for distances in FURTHER:
        pl.semaphore_signal(barrier, inc=1, device_id=away(distances), device_id_type=MESH)

    zero = jnp.zeros((SYS, BS), jnp.float32)
    terms[SLOTS] = zero
    both_c[CODES, 0:SYS] = zero
    both_f[CODES, 0:SYS] = zero

    for load in loads[:4]:
        load.wait()
    halo_a[SELF] = rhs[...]
    codes_g = [pcol[0, k] for k in range(SLOTS)]
    count = ccnt[0, 0, 0]
    codes_h = [ccol[0, k] for k in range(SLOTS)]
    for k in range(SLOTS):
        sel_h[k] = jnp.where(k < count, codes_h[k], CODES)
    codes_h = [sel_h[k] for k in range(SLOTS)]
    for inv, codes in ((inv_g, codes_g), (inv_h, codes_h)):
        for code in NEAR:
            slot = jnp.int32(SLOTS)
            for k in range(1, SLOTS):
                slot = jnp.where(codes[k] == code, k, slot)
            inv[code] = slot

    pl.semaphore_wait(barrier, len(NEAR) + len(FURTHER))

    def exchange(phase, source_of, target):
        for code in NEAR:
            pltpu.make_async_remote_copy(
                src_ref=source_of(code),
                dst_ref=target.at[CODES - 1 - code],
                send_sem=send_sem.at[phase],
                recv_sem=recv_sem.at[phase],
                device_id=near(code),
                device_id_type=MESH,
            ).start()

    def arrived(phase, target, n):
        here = target.at[pl.ds(0, n)]
        pltpu.make_async_copy(here, here, recv_sem.at[phase]).wait()

    def left(phase, target, n):
        here = target.at[pl.ds(0, n)]
        pltpu.make_async_copy(here, here, send_sem.at[phase]).wait()

    def forward(tiles, codes, halo, rows):
        total = None
        for k in range(SLOTS):
            picked = halo[SELF, rows] if k == 0 else halo[codes[k], rows]
            term = dot_fwd(two_parts(picked), tiles[k])
            total = term if total is None else total + term
        return joined(total)

    def backward(tiles, vec):
        pair = two_parts(vec)
        for k in range(1, SLOTS):
            terms[k] = joined(dot_bwd(pair, tiles[k]))
        return joined(dot_bwd(pair, tiles[0]))

    def folded(fold, rows):
        total = None
        for code in NEAR:
            term = fold[code, rows]
            total = term if total is None else total + term
        return total

    def inner(left_vec, right_vec):
        return jnp.sum(left_vec * right_vec, axis=1, keepdims=True)

    everything = slice(0, SYS)
    second = slice(SYS, 2 * SYS)

    def apply_m_tail(vec, halo, send, fold, phase):
        inter = pdia[...] * vec + forward(prec, codes_g, halo, everything)
        own = backward(prec, inter)
        for code in NEAR:
            send[code] = terms[inv_g[code]]
        exchange(phase, lambda code: send.at[code], fold)
        partial = pdia[...] * inter + own
        arrived(phase, fold, CODES - 1)
        return partial + folded(fold, everything)

    def apply_h(vec, send, both, phase):
        own = backward(coup, vec)
        for code in NEAR:
            send[code, everything] = vec
            send[code, second] = terms[inv_h[code]]
        exchange(phase, lambda code: send.at[code], both)
        both[SELF, everything] = vec
        partial = hard[...] * vec + own
        arrived(phase, both, CODES - 1)
        return partial + folded(both, second) + forward(coup, codes_h, both, everything)

    r0 = rhs[...]
    exchange(0, lambda code: rhs, halo_a)
    for load in loads[4:6]:
        load.wait()
    arrived(0, halo_a, CODES - 1)
    z0 = apply_m_tail(r0, halo_a, send_b, fold_b, 1)
    for load in loads[6:]:
        load.wait()
    w0 = apply_h(z0, send_c, both_c, 2)
    send_d[...] = w0
    halo_d[SELF] = w0
    exchange(3, lambda code: send_d, halo_d)
    lane = lax.broadcasted_iota(jnp.int32, (1, 128), 1)

    def placed(row, place, value):
        row = jnp.where(lane == 2 * place, value[0:1], row)
        return jnp.where(lane == 2 * place + 1, value[1:2], row)

    known = placed(jnp.zeros((1, 128), jnp.float32), 0, inner(r0, z0))
    known = placed(known, 1, inner(z0, w0))
    arrived(3, halo_d, CODES - 1)
    y0 = apply_m_tail(w0, halo_d, send_e, fold_e, 4)
    q0 = apply_h(y0, send_f, both_f, 5)
    known = placed(known, 2, inner(w0, y0))
    known = placed(known, 3, inner(r0, y0))
    known = placed(known, 4, inner(y0, q0))

    def summed(phase, total, source, slots, offsets):
        source[...] = total
        for place, distances in enumerate(offsets):
            pltpu.make_async_remote_copy(
                src_ref=source,
                dst_ref=slots.at[place],
                send_sem=send_sem.at[phase],
                recv_sem=recv_sem.at[phase],
                device_id=away(distances),
                device_id_type=MESH,
            ).start()
        arrived(phase, slots, len(offsets))
        return total + jnp.sum(slots[...], axis=0)

    plane = [(0, b, c) for b in range(sizes[1]) for c in range(sizes[2])][1:]
    ring = [(a, 0, 0) for a in range(1, sizes[0])]
    total = summed(6, known, parts, part_plane, plane)
    total = summed(7, total, sums_plane, part_ring, ring)

    row = lax.broadcasted_iota(jnp.int32, (SYS, BS), 0)
    rz0, c0, wy, ry, yq = (
        jnp.where(row == 0, total[:, 2 * i : 2 * i + 1], total[:, 2 * i + 1 : 2 * i + 2]) for i in range(SUMS)
    )
    alpha = rz0 / c0
    rz1 = rz0 - alpha * (ry + c0) + alpha * alpha * wy
    scale = 1.0 + rz1 / rz0
    c1 = scale * scale * c0 - 2.0 * alpha * scale * wy + alpha * alpha * yq
    alpha1 = rz1 / c1
    charges[...] = alpha * z0 + alpha1 * (scale * z0 - alpha * y0)
    resid[...] = r0 - alpha * w0 - alpha1 * (scale * w0 - alpha * q0)
    for phase, target in ((0, halo_a), (1, fold_b), (2, both_c), (3, halo_d), (4, fold_e), (5, both_f)):
        left(phase, target, CODES - 1)
    for phase, target in ((6, part_plane), (7, part_ring)):
        left(phase, target, target.shape[0])


def finish(charges, residual, charges_out, residual_out, sem):
    copies = [
        pltpu.make_async_copy(charges, charges_out, sem.at[0]),
        pltpu.make_async_copy(residual, residual_out, sem.at[1]),
    ]
    for copy in copies:
        copy.start()
    for copy in copies:
        copy.wait()


def body(sizes, right_side, hardness, coupling, coupling_cols, coupling_count, precond_diag, precond, precond_cols):
    f32, i32, bf16 = jnp.float32, jnp.int32, jnp.bfloat16
    vec = jax.ShapeDtypeStruct((SYS, BS), f32)
    slots = lambda n, rows=SYS: pltpu.VMEM((n, rows, BS), f32)
    anywhere = pl.BlockSpec(memory_space=pl.ANY)

    def run(*refs):
        kernel(sizes, *refs)

    charges, residual = pl.pallas_call(
        run,
        out_shape=(pltpu.VMEM((SYS, BS), f32),) * 2,
        in_specs=[anywhere] * 8,
        out_specs=(pl.BlockSpec(memory_space=pltpu.VMEM),)*2,
        scratch_shapes=[
            pltpu.VMEM((SYS, BS), f32), pltpu.VMEM((1, BS), f32), pltpu.VMEM((SLOTS, BS, BS), bf16),
            pltpu.VMEM((1, BS), f32), pltpu.VMEM((SLOTS, BS, BS), bf16),
            pltpu.SMEM((1, SLOTS), i32), pltpu.SMEM((1, 1, 1), i32), pltpu.SMEM((1, SLOTS), i32),
            pltpu.SMEM((CODES,), i32), pltpu.SMEM((CODES,), i32), pltpu.SMEM((SLOTS,), i32),
            slots(CODES), slots(CODES), slots(CODES), slots(CODES, 2 * SYS), slots(CODES + 1, 2 * SYS),
            pltpu.VMEM((SYS, BS), f32), slots(CODES), slots(CODES), slots(CODES), slots(CODES, 2 * SYS), slots(CODES + 1, 2 * SYS),
            pltpu.VMEM((1, 128), f32), pltpu.VMEM((sizes[1] * sizes[2] - 1, 1, 128), f32),
            pltpu.VMEM((sizes[0] - 1, 1, 128), f32), pltpu.VMEM((1, 128), f32),
            slots(SLOTS + 1),
            pltpu.SemaphoreType.DMA((8,)), pltpu.SemaphoreType.DMA((8,)), pltpu.SemaphoreType.DMA((8,)),
        ],
        compiler_params=pltpu.CompilerParams(
            collective_id=0, has_side_effects=True, vmem_limit_bytes=56 * 1024 * 1024
        ),
    )(
        right_side.reshape(SYS, BS), hardness.reshape(1, BS), coupling.reshape(SLOTS, BS, BS),
        coupling_cols.reshape(1, SLOTS), coupling_count, precond_diag.reshape(1, BS),
        precond.reshape(SLOTS, BS, BS), precond_cols.reshape(1, SLOTS),
    )
    charges, residual = pl.pallas_call(
        finish,
        out_shape=(vec, vec),
        in_specs=[anywhere] * 2,
        out_specs=(anywhere, anywhere),
        scratch_shapes=[pltpu.SemaphoreType.DMA((2,))],
    )(charges, residual)
    return charges.reshape(right_side.shape), residual.reshape(right_side.shape)


def solution(mesh):
    sizes = tuple(mesh.shape[a] for a in AXES)
    placed = (
        P("gx", "gy", "gz", None, None),
        P("gx", "gy", "gz", None),
        P("gx", "gy", "gz", None, None, None),
        P("gx", "gy", "gz", None),
        P("gx", "gy", "gz"),
        P("gx", "gy", "gz", None),
        P("gx", "gy", "gz", None, None, None),
        P("gx", "gy", "gz", None),
    )
    return jax.shard_map(
        lambda *args: body(sizes, *args),
        mesh=mesh,
        in_specs=placed,
        out_specs=(P("gx", "gy", "gz", None, None), P("gx", "gy", "gz", None, None)),
        check_vma=False,
    )
```

time: 77.8 us -> 69.2 us (0.89)
  Pallas kernels: 72.1 us -> 66.6 us
  local copies, waits for them, and re-layouts: 4.11 us -> 1.13 us
    pallas_call x1 -> x2, Pallas kernels: 72.1 us -> 66.6 us  [the longest x1 65.3 us: body(): pl.pallas_call(run, out_shape=(pltpu.VMEM((SYS, BS), f32),) * 2, in_specs...]
    unnamed x16 -> x4, local copies, waits for them, and re-layouts: 4.11 us -> 1.13 us
where the time goes in v2:
time: 69.2 us; the launch traced here: 69 us
  Pallas kernels  66.6 us (96%)
  between operations  1.29 us (2%)
  local copies, waits for them, and re-layouts  1.13 us (2%)
    pallas_call x1, Pallas kernels, body(): pl.pallas_call(run, out_shape=(pltpu.VMEM((SYS, BS), f32),) * 2, in_specs...  65.3 us

profile of v2, /device:TPU:1, one launch (start us, length us, event | category | flops | bytes accessed | tf_op | source)
XLA Modules:
  0.0 69.0 jit_solution(9299212317843478901)
XLA Ops:
  1.3 65.3 %shard_map.95 = (f32[2,256]{1,0:T(2,128)S(1)}, f32[2,256]{1,0:T(2,128)S(1)}) custom-call(f32[2,256]{1,0:T(2,128)} %bitcast.11, f32[1,256]{1,0:T(1,128)} %bitcast.12, bf16[6,256,256]{2,1,0:T(8,128)(2,1)} %bitcast.9, s32[1,6]{1,0:T(1,128)} %bitcast.14, s32[1,1,1]{2,1,0:T(1,128)S(6)} %copy.10.refs_4_, f32[1,256]{1,0:T(1,128)} %bitcast.13, ...), custom_call_target="tpu_custom_call" | custom-call | tf_op jit(solution)/shard_map/pallas_call | solution.py:255
  66.6 0.0 copy-start
  66.6 0.6 copy-done
  67.2 0.0 copy-start.1
  67.2 0.6 copy-done.1
  67.8 1.2 %shard_map.96 = (f32[2,256]{1,0:T(2,128)}, f32[2,256]{1,0:T(2,128)}) custom-call(f32[2,256]{1,0:T(2,128)} %copy-done, f32[2,256]{1,0:T(2,128)} %copy-done.1), custom_call_target="tpu_custom_call" | custom-call | tf_op jit(solution)/shard_map/pallas_call | solution.py:280
Async XLA Ops:
  66.6 0.6 copy-start
  67.2 0.6 copy-start.1

commit v3 on v2

--- a/solution.py
+++ b/solution.py
@@ -29,6 +29,13 @@
 
 def joined(product):
     return product[0:SYS] + product[SYS : 2 * SYS]
+
+
+def tree_sum(terms):
+    while len(terms) > 1:
+        half = len(terms) // 2
+        terms = [a + b for a, b in zip(terms[:half], terms[half : 2 * half])] + terms[2 * half :]
+    return terms[0]
 
 
 def dot_fwd(vec, tile):
@@ -70,23 +77,95 @@
             (prec_hbm, prec), (hard_hbm, hard), (coup_hbm, coup),
         ))
     ]
-    for load in loads:
-        load.start()
 
     barrier = pltpu.get_barrier_semaphore()
     for code in NEAR:
         pl.semaphore_signal(barrier, inc=1, device_id=near(code), device_id_type=MESH)
     for distances in FURTHER:
         pl.semaphore_signal(barrier, inc=1, device_id=away(distances), device_id_type=MESH)
+    for load in loads:
+        load.start()
 
     zero = jnp.zeros((SYS, BS), jnp.float32)
     terms[SLOTS] = zero
     both_c[CODES, 0:SYS] = zero
     both_f[CODES, 0:SYS] = zero
 
-    for load in loads[:4]:
+    loads[0].wait()
+    halo_a[SELF] = rhs[...]
+    pl.semaphore_wait(barrier, len(NEAR) + len(FURTHER))
+
+    def exchange(phase, source_of, target):
+        for code in NEAR:
+            pltpu.make_async_remote_copy(
+                src_ref=source_of(code),
+                dst_ref=target.at[CODES - 1 - code],
+                send_sem=send_sem.at[phase],
+                recv_sem=recv_sem.at[phase],
+                device_id=near(code),
+                device_id_type=MESH,
+            ).start()
+
+    def arrived(phase, target, n):
+        here = target.at[pl.ds(0, n)]
+        pltpu.make_async_copy(here, here, recv_sem.at[phase]).wait()
+
+    def left(phase, target, n):
+        here = target.at[pl.ds(0, n)]
+        pltpu.make_async_copy(here, here, send_sem.at[phase]).wait()
+
+    def forward(tiles, codes, halo, rows):
+        total = None
+        for k in range(SLOTS):
+            picked = halo[SELF, rows] if k == 0 else halo[codes[k], rows]
+            term = dot_fwd(two_parts(picked), tiles[k])
+            total = term if total is None else total + term
+        return joined(total)
+
+    def backward(tiles, vec):
+        pair = two_parts(vec)
+        for k in range(1, SLOTS):
+            terms[k] = joined(dot_bwd(pair, tiles[k]))
+        return joined(dot_bwd(pair, tiles[0]))
+
+    def folded(fold, rows):
+        return tree_sum([fold[code, rows] for code in NEAR])
+
+    def inner(left_vec, right_vec):
+        return jnp.sum(left_vec * right_vec, axis=1, keepdims=True)
+
+    everything = slice(0, SYS)
+    second = slice(SYS, 2 * SYS)
+
+    def apply_m_tail(vec, halo, send, fold, phase):
+        inter = pdia[...] * vec + forward(prec, codes_g, halo, everything)
+        own = backward(prec, inter)
+        for code in NEAR:
+            send[code] = terms[inv_g[code]]
+        exchange(phase, lambda code: send.at[code], fold)
+        partial = pdia[...] * inter + own
+        arrived(phase, fold, CODES - 1)
+        return partial + folded(fold, everything)
+
+    def apply_h_start(vec, send, both, phase):
+        own = backward(coup, vec)
+        for code in NEAR:
+            send[code, everything] = vec
+            send[code, second] = terms[inv_h[code]]
+        exchange(phase, lambda code: send.at[code], both)
+        both[SELF, everything] = vec
+        return own
+
+    def apply_h(vec, send, both, phase):
+        own = apply_h_start(vec, send, both, phase)
+        partial = hard[...] * vec + own
+        arrived(phase, both, CODES - 1)
+        return partial + folded(both, second) + forward(coup, codes_h, both, everything)
+
+    r0 = rhs[...]
+    exchange(0, lambda code: rhs, halo_a)
+    for load in loads[1:4]:
         load.wait()
-    halo_a[SELF] = rhs[...]
     codes_g = [pcol[0, k] for k in range(SLOTS)]
     count = ccnt[0, 0, 0]
     codes_h = [ccol[0, k] for k in range(SLOTS)]
@@ -100,77 +179,6 @@
                 slot = jnp.where(codes[k] == code, k, slot)
             inv[code] = slot
 
-    pl.semaphore_wait(barrier, len(NEAR) + len(FURTHER))
-
-    def exchange(phase, source_of, target):
-        for code in NEAR:
-            pltpu.make_async_remote_copy(
-                src_ref=source_of(code),
-                dst_ref=target.at[CODES - 1 - code],
-                send_sem=send_sem.at[phase],
-                recv_sem=recv_sem.at[phase],
-                device_id=near(code),
-                device_id_type=MESH,
-            ).start()
-
-    def arrived(phase, target, n):
-        here = target.at[pl.ds(0, n)]
-        pltpu.make_async_copy(here, here, recv_sem.at[phase]).wait()
-
-    def left(phase, target, n):
-        here = target.at[pl.ds(0, n)]
-        pltpu.make_async_copy(here, here, send_sem.at[phase]).wait()
-
-    def forward(tiles, codes, halo, rows):
-        total = None
-        for k in range(SLOTS):
-            picked = halo[SELF, rows] if k == 0 else halo[codes[k], rows]
-            term = dot_fwd(two_parts(picked), tiles[k])
-            total = term if total is None else total + term
-        return joined(total)
-
-    def backward(tiles, vec):
-        pair = two_parts(vec)
-        for k in range(1, SLOTS):
-            terms[k] = joined(dot_bwd(pair, tiles[k]))
-        return joined(dot_bwd(pair, tiles[0]))
-
-    def folded(fold, rows):
-        total = None
-        for code in NEAR:
-            term = fold[code, rows]
-            total = term if total is None else total + term
-        return total
-
-    def inner(left_vec, right_vec):
-        return jnp.sum(left_vec * right_vec, axis=1, keepdims=True)
-
-    everything = slice(0, SYS)
-    second = slice(SYS, 2 * SYS)
-
-    def apply_m_tail(vec, halo, send, fold, phase):
-        inter = pdia[...] * vec + forward(prec, codes_g, halo, everything)
-        own = backward(prec, inter)
-        for code in NEAR:
-            send[code] = terms[inv_g[code]]
-        exchange(phase, lambda code: send.at[code], fold)
-        partial = pdia[...] * inter + own
-        arrived(phase, fold, CODES - 1)
-        return partial + folded(fold, everything)
-
-    def apply_h(vec, send, both, phase):
-        own = backward(coup, vec)
-        for code in NEAR:
-            send[code, everything] = vec
-            send[code, second] = terms[inv_h[code]]
-        exchange(phase, lambda code: send.at[code], both)
-        both[SELF, everything] = vec
-        partial = hard[...] * vec + own
-        arrived(phase, both, CODES - 1)
-        return partial + folded(both, second) + forward(coup, codes_h, both, everything)
-
-    r0 = rhs[...]
-    exchange(0, lambda code: rhs, halo_a)
     for load in loads[4:6]:
         load.wait()
     arrived(0, halo_a, CODES - 1)
@@ -191,12 +199,15 @@
     known = placed(known, 1, inner(z0, w0))
     arrived(3, halo_d, CODES - 1)
     y0 = apply_m_tail(w0, halo_d, send_e, fold_e, 4)
-    q0 = apply_h(y0, send_f, both_f, 5)
+    own = apply_h_start(y0, send_f, both_f, 5)
     known = placed(known, 2, inner(w0, y0))
     known = placed(known, 3, inner(r0, y0))
-    known = placed(known, 4, inner(y0, q0))
-
-    def summed(phase, total, source, slots, offsets):
+    scaled = hard[...] * y0
+    arrived(5, both_f, CODES - 1)
+    back = own + folded(both_f, second)
+    known = placed(known, 4, inner(y0, scaled + 2.0 * back))
+
+    def spread(phase, total, source, slots, offsets):
         source[...] = total
         for place, distances in enumerate(offsets):
             pltpu.make_async_remote_copy(
@@ -207,13 +218,21 @@
                 device_id=away(distances),
                 device_id_type=MESH,
             ).start()
+
+    def summed(phase, total, slots, offsets):
         arrived(phase, slots, len(offsets))
-        return total + jnp.sum(slots[...], axis=0)
+        return tree_sum([total] + [slots[place] for place in range(len(offsets))])
 
     plane = [(0, b, c) for b in range(sizes[1]) for c in range(sizes[2])][1:]
     ring = [(a, 0, 0) for a in range(1, sizes[0])]
-    total = summed(6, known, parts, part_plane, plane)
-    total = summed(7, total, sums_plane, part_ring, ring)
+    spread(6, known, parts, part_plane, plane)
+    q0 = scaled + back + forward(coup, codes_h, both_f, everything)
+    total = summed(6, known, part_plane, plane)
+    spread(7, total, sums_plane, part_ring, ring)
+    for phase, target in ((0, halo_a), (1, fold_b), (2, both_c), (3, halo_d), (4, fold_e), (5, both_f)):
+        left(phase, target, CODES - 1)
+    left(6, part_plane, len(plane))
+    total = summed(7, total, part_ring, ring)
 
     row = lax.broadcasted_iota(jnp.int32, (SYS, BS), 0)
     rz0, c0, wy, ry, yq = (
@@ -226,10 +245,7 @@
     alpha1 = rz1 / c1
     charges[...] = alpha * z0 + alpha1 * (scale * z0 - alpha * y0)
     resid[...] = r0 - alpha * w0 - alpha1 * (scale * w0 - alpha * q0)
-    for phase, target in ((0, halo_a), (1, fold_b), (2, both_c), (3, halo_d), (4, fold_e), (5, both_f)):
-        left(phase, target, CODES - 1)
-    for phase, target in ((6, part_plane), (7, part_ring)):
-        left(phase, target, target.shape[0])
+    left(7, part_ring, len(ring))
 
 
 def finish(charges, residual, charges_out, residual_out, sem):
@@ -256,7 +272,7 @@
         run,
         out_shape=(pltpu.VMEM((SYS, BS), f32),) * 2,
         in_specs=[anywhere] * 8,
-        out_specs=(pl.BlockSpec(memory_space=pltpu.VMEM),)*2,
+        out_specs=(pl.BlockSpec(memory_space=pltpu.VMEM),) * 2,
         scratch_shapes=[
             pltpu.VMEM((SYS, BS), f32), pltpu.VMEM((1, BS), f32), pltpu.VMEM((SLOTS, BS, BS), bf16),
             pltpu.VMEM((1, BS), f32), pltpu.VMEM((SLOTS, BS, BS), bf16),
@@ -283,6 +299,7 @@
         in_specs=[anywhere] * 2,
         out_specs=(anywhere, anywhere),
         scratch_shapes=[pltpu.SemaphoreType.DMA((2,))],
+        compiler_params=pltpu.CompilerParams(vmem_limit_bytes=1024 * 1024),
     )(charges, residual)
     return charges.reshape(right_side.shape), residual.reshape(right_side.shape)
 

time: 69.2 us -> 66.8 us (0.965)
  Pallas kernels: 66.6 us -> 65.3 us
  local copies, waits for them, and re-layouts: 1.13 us -> 0 us
    unnamed x4 -> x0, local copies, waits for them, and re-layouts: 1.13 us -> none
where the time goes in v3:
time: 66.8 us; the launch traced here: 66.6 us
  Pallas kernels  65.3 us (98%)
  between operations  1.29 us (2%)
    pallas_call x1, Pallas kernels, body(): pl.pallas_call(run, out_shape=(pltpu.VMEM((SYS, BS), f32),) * 2, in_specs...  64.7 us

profile of v3, /device:TPU:1, one launch (start us, length us, event | category | flops | bytes accessed | tf_op | source)
XLA Modules:
  0.0 66.6 jit_solution(10003277173294142694)
XLA Ops:
  1.3 64.7 %shard_map.95 = (f32[2,256]{1,0:T(2,128)S(1)}, f32[2,256]{1,0:T(2,128)S(1)}) custom-call(f32[2,256]{1,0:T(2,128)} %bitcast.11, f32[1,256]{1,0:T(1,128)} %bitcast.12, bf16[6,256,256]{2,1,0:T(8,128)(2,1)} %bitcast.9, s32[1,6]{1,0:T(1,128)} %bitcast.14, s32[1,1,1]{2,1,0:T(1,128)S(6)} %copy.10.refs_4_, f32[1,256]{1,0:T(1,128)} %bitcast.13, ...), custom_call_target="tpu_custom_call" | custom-call | tf_op jit(solution)/shard_map/pallas_call | solution.py:271
  66.0 0.6 shard_map.96

commit v4 on v3

--- a/solution.py
+++ b/solution.py
@@ -38,11 +38,7 @@
     return terms[0]
 
 
-def dot_fwd(vec, tile):
-    return lax.dot_general(vec, tile, (((1,), (1,)), ((), ())), preferred_element_type=jnp.float32)
-
-
-def dot_bwd(vec, tile):
+def dot(vec, tile):
     return lax.dot_general(vec, tile, (((1,), (0,)), ((), ())), preferred_element_type=jnp.float32)
 
 
@@ -54,7 +50,7 @@
     inv_g, inv_h, sel_h,
     halo_a, send_b, fold_b, send_c, both_c, send_d, halo_d, send_e, fold_e, send_f, both_f,
     parts, part_plane, part_ring, sums_plane,
-    terms,
+    terms, coup_t, prec_t,
     load_sem, send_sem, recv_sem,
 ):
     me = [lax.axis_index(a) for a in AXES]
@@ -114,19 +110,23 @@
         here = target.at[pl.ds(0, n)]
         pltpu.make_async_copy(here, here, send_sem.at[phase]).wait()
 
-    def forward(tiles, codes, halo, rows):
+    def turn(tiles, turned):
+        for k in range(SLOTS):
+            turned[k] = tiles[k].T
+
+    def forward(turned, codes, halo, rows):
         total = None
         for k in range(SLOTS):
             picked = halo[SELF, rows] if k == 0 else halo[codes[k], rows]
-            term = dot_fwd(two_parts(picked), tiles[k])
+            term = dot(two_parts(picked), turned[k])
             total = term if total is None else total + term
         return joined(total)
 
     def backward(tiles, vec):
         pair = two_parts(vec)
         for k in range(1, SLOTS):
-            terms[k] = joined(dot_bwd(pair, tiles[k]))
-        return joined(dot_bwd(pair, tiles[0]))
+            terms[k] = joined(dot(pair, tiles[k]))
+        return joined(dot(pair, tiles[0]))
 
     def folded(fold, rows):
         return tree_sum([fold[code, rows] for code in NEAR])
@@ -137,13 +137,15 @@
     everything = slice(0, SYS)
     second = slice(SYS, 2 * SYS)
 
-    def apply_m_tail(vec, halo, send, fold, phase):
-        inter = pdia[...] * vec + forward(prec, codes_g, halo, everything)
+    def apply_m_tail(vec, halo, send, fold, phase, meanwhile=None):
+        inter = pdia[...] * vec + forward(prec_t, codes_g, halo, everything)
         own = backward(prec, inter)
         for code in NEAR:
             send[code] = terms[inv_g[code]]
         exchange(phase, lambda code: send.at[code], fold)
         partial = pdia[...] * inter + own
+        if meanwhile is not None:
+            meanwhile()
         arrived(phase, fold, CODES - 1)
         return partial + folded(fold, everything)
 
@@ -160,7 +162,7 @@
         own = apply_h_start(vec, send, both, phase)
         partial = hard[...] * vec + own
         arrived(phase, both, CODES - 1)
-        return partial + folded(both, second) + forward(coup, codes_h, both, everything)
+        return partial + folded(both, second) + forward(coup_t, codes_h, both, everything)
 
     r0 = rhs[...]
     exchange(0, lambda code: rhs, halo_a)
@@ -181,10 +183,15 @@
 
     for load in loads[4:6]:
         load.wait()
+    turn(prec, prec_t)
     arrived(0, halo_a, CODES - 1)
-    z0 = apply_m_tail(r0, halo_a, send_b, fold_b, 1)
-    for load in loads[6:]:
-        load.wait()
+
+    def ready_coupling():
+        for load in loads[6:]:
+            load.wait()
+        turn(coup, coup_t)
+
+    z0 = apply_m_tail(r0, halo_a, send_b, fold_b, 1, ready_coupling)
     w0 = apply_h(z0, send_c, both_c, 2)
     send_d[...] = w0
     halo_d[SELF] = w0
@@ -223,10 +230,14 @@
         arrived(phase, slots, len(offsets))
         return tree_sum([total] + [slots[place] for place in range(len(offsets))])
 
-    plane = [(0, b, c) for b in range(sizes[1]) for c in range(sizes[2])][1:]
-    ring = [(a, 0, 0) for a in range(1, sizes[0])]
+    def hops(distances):
+        x, y, z = (min(d, n - d) for d, n in zip(distances, sizes))
+        return -(x + y + z / 2)
+
+    plane = sorted([(0, b, c) for b in range(sizes[1]) for c in range(sizes[2])][1:], key=hops)
+    ring = sorted([(a, 0, 0) for a in range(1, sizes[0])], key=hops)
     spread(6, known, parts, part_plane, plane)
-    q0 = scaled + back + forward(coup, codes_h, both_f, everything)
+    q0 = scaled + back + forward(coup_t, codes_h, both_f, everything)
     total = summed(6, known, part_plane, plane)
     spread(7, total, sums_plane, part_ring, ring)
     for phase, target in ((0, halo_a), (1, fold_b), (2, both_c), (3, halo_d), (4, fold_e), (5, both_f)):
@@ -282,7 +293,7 @@
             pltpu.VMEM((SYS, BS), f32), slots(CODES), slots(CODES), slots(CODES), slots(CODES, 2 * SYS), slots(CODES + 1, 2 * SYS),
             pltpu.VMEM((1, 128), f32), pltpu.VMEM((sizes[1] * sizes[2] - 1, 1, 128), f32),
             pltpu.VMEM((sizes[0] - 1, 1, 128), f32), pltpu.VMEM((1, 128), f32),
-            slots(SLOTS + 1),
+            slots(SLOTS + 1), pltpu.VMEM((SLOTS, BS, BS), bf16), pltpu.VMEM((SLOTS, BS, BS), bf16),
             pltpu.SemaphoreType.DMA((8,)), pltpu.SemaphoreType.DMA((8,)), pltpu.SemaphoreType.DMA((8,)),
         ],
         compiler_params=pltpu.CompilerParams(

time: 66.8 us -> 66 us (0.988)
  Pallas kernels: 65.3 us -> 64.5 us
    pallas_call x1, Pallas kernels: 64.7 us -> 63.9 us  [body(): pl.pallas_call(run, out_shape=(pltpu.VMEM((SYS, BS), f32),) * 2, in_specs...]
where the time goes in v4:
time: 66 us; the launch traced here: 65.8 us
  Pallas kernels  64.5 us (98%)
  between operations  1.29 us (2%)
    pallas_call x1, Pallas kernels, body(): pl.pallas_call(run, out_shape=(pltpu.VMEM((SYS, BS), f32),) * 2, in_specs...  63.9 us

profile of v4, /device:TPU:1, one launch (start us, length us, event | category | flops | bytes accessed | tf_op | source)
XLA Modules:
  0.0 65.8 jit_solution(15161349615789223075)
XLA Ops:
  1.3 63.9 %shard_map.95 = (f32[2,256]{1,0:T(2,128)S(1)}, f32[2,256]{1,0:T(2,128)S(1)}) custom-call(f32[2,256]{1,0:T(2,128)} %bitcast.11, f32[1,256]{1,0:T(1,128)} %bitcast.12, bf16[6,256,256]{2,1,0:T(8,128)(2,1)} %bitcast.9, s32[1,6]{1,0:T(1,128)} %bitcast.14, s32[1,1,1]{2,1,0:T(1,128)S(6)} %copy.10.refs_4_, f32[1,256]{1,0:T(1,128)} %bitcast.13, ...), custom_call_target="tpu_custom_call" | custom-call | tf_op jit(solution)/shard_map/pallas_call | solution.py:282
  65.2 0.6 shard_map.96

commit v5 on v4

--- a/solution.py
+++ b/solution.py
@@ -12,12 +12,11 @@
 SELF = 13
 AXES = ("gx", "gy", "gz")
 MESH = pl.DeviceIdType.MESH
+OVER, BESIDE = 1, 2
 NEAR = sorted(
-    (o for o in range(CODES) if o != SELF),
-    key=lambda o: -(abs(o // 9 - 1) + abs(o // 3 % 3 - 1) + abs(o % 3 - 1)),
+    ((x, y, t) for x in (-1, 0, 1) for y in (-1, 0, 1) for t in (0, OVER, BESIDE) if (x, y, t) != (0, 0, 0)),
+    key=lambda o: -(4 * (abs(o[0]) + abs(o[1]) + (o[2] == OVER)) + (o[2] == BESIDE)),
 )
-
-
 FURTHER = ((-2, 0, 0), (2, 0, 0), (0, 0, -2), (0, 0, 2))
 SUMS = 5
 
@@ -57,9 +56,19 @@
     steps = [
         [lax.rem(me[a] + (n - 1), n), me[a], lax.rem(me[a] + 1, n)] for a, n in enumerate(sizes)
     ]
-
-    def near(code):
-        return (steps[0][code // 9], steps[1][code // 3 % 3], steps[2][code % 3])
+    core = lax.rem(me[2], 2)
+    thirds = [1, 2 * core, 2 - 2 * core]
+    leads = [
+        me[2],
+        lax.rem(me[2] + (sizes[2] - 1) + 2 * core, sizes[2]),
+        me[2] + 1 - 2 * core,
+    ]
+
+    def code_of(o):
+        return (o[0] + 1) * 9 + (o[1] + 1) * 3 + thirds[o[2]]
+
+    def near(o):
+        return (steps[0][o[0] + 1], steps[1][o[1] + 1], leads[o[2]])
 
     def away(distances):
         return tuple(
@@ -75,8 +84,8 @@
     ]
 
     barrier = pltpu.get_barrier_semaphore()
-    for code in NEAR:
-        pl.semaphore_signal(barrier, inc=1, device_id=near(code), device_id_type=MESH)
+    for offset in NEAR:
+        pl.semaphore_signal(barrier, inc=1, device_id=near(offset), device_id_type=MESH)
     for distances in FURTHER:
         pl.semaphore_signal(barrier, inc=1, device_id=away(distances), device_id_type=MESH)
     for load in loads:
@@ -92,13 +101,14 @@
     pl.semaphore_wait(barrier, len(NEAR) + len(FURTHER))
 
     def exchange(phase, source_of, target):
-        for code in NEAR:
+        for offset in NEAR:
+            code = code_of(offset)
             pltpu.make_async_remote_copy(
                 src_ref=source_of(code),
                 dst_ref=target.at[CODES - 1 - code],
                 send_sem=send_sem.at[phase],
                 recv_sem=recv_sem.at[phase],
-                device_id=near(code),
+                device_id=near(offset),
                 device_id_type=MESH,
             ).start()
 
@@ -129,7 +139,7 @@
         return joined(dot(pair, tiles[0]))
 
     def folded(fold, rows):
-        return tree_sum([fold[code, rows] for code in NEAR])
+        return tree_sum([fold[code, rows] for code in range(CODES) if code != SELF])
 
     def inner(left_vec, right_vec):
         return jnp.sum(left_vec * right_vec, axis=1, keepdims=True)
@@ -140,7 +150,7 @@
     def apply_m_tail(vec, halo, send, fold, phase, meanwhile=None):
         inter = pdia[...] * vec + forward(prec_t, codes_g, halo, everything)
         own = backward(prec, inter)
-        for code in NEAR:
+        for code in range(CODES):
             send[code] = terms[inv_g[code]]
         exchange(phase, lambda code: send.at[code], fold)
         partial = pdia[...] * inter + own
@@ -151,7 +161,7 @@
 
     def apply_h_start(vec, send, both, phase):
         own = backward(coup, vec)
-        for code in NEAR:
+        for code in range(CODES):
             send[code, everything] = vec
             send[code, second] = terms[inv_h[code]]
         exchange(phase, lambda code: send.at[code], both)
@@ -175,7 +185,7 @@
         sel_h[k] = jnp.where(k < count, codes_h[k], CODES)
     codes_h = [sel_h[k] for k in range(SLOTS)]
     for inv, codes in ((inv_g, codes_g), (inv_h, codes_h)):
-        for code in NEAR:
+        for code in range(CODES):
             slot = jnp.int32(SLOTS)
             for k in range(1, SLOTS):
                 slot = jnp.where(codes[k] == code, k, slot)

time: 66 us -> 65.8 us (level)
  no operation moved by 1% of the time
where the time goes in v5:
time: 65.8 us; the launch traced here: 65.6 us
  Pallas kernels  64.3 us (98%)
  between operations  1.29 us (2%)
    pallas_call x1, Pallas kernels, body(): pl.pallas_call(run, out_shape=(pltpu.VMEM((SYS, BS), f32),) * 2, in_specs...  63.7 us

profile of v5, /device:TPU:1, one launch (start us, length us, event | category | flops | bytes accessed | tf_op | source)
XLA Modules:
  0.0 65.6 jit_solution(7286975084006342367)
XLA Ops:
  1.3 63.7 %shard_map.95 = (f32[2,256]{1,0:T(2,128)S(1)}, f32[2,256]{1,0:T(2,128)S(1)}) custom-call(f32[2,256]{1,0:T(2,128)} %bitcast.11, f32[1,256]{1,0:T(1,128)} %bitcast.12, bf16[6,256,256]{2,1,0:T(8,128)(2,1)} %bitcast.9, s32[1,6]{1,0:T(1,128)} %bitcast.14, s32[1,1,1]{2,1,0:T(1,128)S(6)} %copy.10.refs_4_, f32[1,256]{1,0:T(1,128)} %bitcast.13, ...), custom_call_target="tpu_custom_call" | custom-call | tf_op jit(solution)/shard_map/pallas_call | solution.py:292
  65.0 0.6 shard_map.96
